TPU v7x, 32 devices: a whole 2x2x4 slice. The times are simulated.
32 devices in a mesh: tm: 8 (over y, x, core), space: 4 (over z).
Axes of the slice: x: 2, y: 2, z: 4, core: 2. Of those that a mesh axis runs over, the one named last changes fastest.
Arguments:
- state: float32 [16, 1024, 256], P('tm', 'space'), may hold values from -6 to 6
- forcing: float32 [16, 1024, 256], P('tm', 'space'), may hold values from -6 to 6
- jscale: float32 [1024], P('space'), may hold values from 0.5 to 2
- volume_kernel: float32 [256, 256], replicated, may hold values from -0.375 to 0.375
- neighbour: int32 [1024, 6], P('space'), may hold values from 0 to 383, as said below
- send_left: int32 [256], P('space'), may hold values from 0 to 255, as said below
- send_right: int32 [256], P('space'), may hold values from 0 to 255, as said below
Outputs:
- residual: float32 [16, 1024, 256], P('tm', 'space')
- new_state: float32 [16, 1024, 256], P('tm', 'space')
Inputs may be any that keep to these rules, and one draw needn't show every extreme that they name: `neighbour`: entries of face 2 are below 320, those of face 3 are below 256 or at least 320, those of the other faces are below 256. `send_left`: each partition's 64 entries are different element numbers. `send_right`: each partition's 64 entries are different element numbers.
All inputs are finite; a program needn't handle non-finite values.
Results may differ from a plain program's by a relative error of at most 0.0003.
Values sent between devices are 32-bit elements; how exact they have to be, the bound alone decides.
A program may use at most 128 MiB of HBM per device.

v0:
```python
import jax
import jax.numpy as jnp
import numpy as np
from jax import lax
from jax.sharding import PartitionSpec as P

lift_factor = 2.0
step_factor = 0.2


def shifted(block, axis, distance):
    devices = range(lax.axis_size(axis))
    route = [((i - distance) % len(devices), i) for i in devices]
    return lax.ppermute(block, axis, route)


def spectral(offset, instances):
    lag_value = offset.astype(jnp.float32)
    parity = 1.0 - 2.0 * jnp.mod(offset, 2).astype(jnp.float32)
    angle_value = jnp.pi * lag_value / instances
    safe_sine = jnp.where(offset == 0, 1.0, jnp.sin(angle_value))
    return jnp.where(offset == 0, 0.0, 0.5 * parity * jnp.cos(angle_value) / safe_sine)


def face_table():
    table = np.zeros((256, 384), np.float32)
    for face_number in range(6):
        node_index = 3 if face_number % 2 else 0
        normal_axis = face_number // 2
        for comp_id in range(4):
            for first in range(4):
                for second in range(4):
                    if normal_axis == 0:
                        nodes = (node_index, first, second)
                    elif normal_axis == 1:
                        nodes = (first, node_index, second)
                    else:
                        nodes = (first, second, node_index)
                    source = comp_id * 64 + nodes[0] * 16 + nodes[1] * 4 + nodes[2]
                    target = face_number * 64 + comp_id * 16 + first * 4 + second
                    table[source, target] = 1.0
    return table


def select_face(blocks, table, face_number):
    columns = table[:, face_number * 64 : (face_number + 1) * 64]
    return jnp.einsum("iek,kl->iel", blocks, columns, precision=lax.Precision.HIGHEST)


def numerical_flux_penalty(minus, exterior_trace, face_number):
    jump_value = exterior_trace - minus
    normal_sign = 1.0 if face_number % 2 else -1.0
    normal_axis = face_number // 2
    pieces = [-0.5 * jump_value[..., 16 * comp_id : 16 * comp_id + 16] for comp_id in range(4)]
    velocity_jump = jump_value[..., 16 * (1 + normal_axis) : 16 * (2 + normal_axis)]
    pressure_jump = jump_value[..., 0:16]
    pieces[0] = pieces[0] + 0.5 * normal_sign * velocity_jump
    pieces[1 + normal_axis] = pieces[1 + normal_axis] + 0.5 * normal_sign * pressure_jump
    return jnp.concatenate(pieces, axis=-1)


def spatial_term(blocks, element_scale, table_rows, halo_left, halo_right, volume_kernel, table):
    local_count = blocks.shape[0]
    halo_count = halo_left.shape[1]
    joined = jnp.concatenate([volume_kernel, table], axis=1)
    product = jnp.einsum("iek,kl->iel", blocks, joined, precision=lax.Precision.HIGHEST)
    volume = product[..., :256]
    trace_values = [
        product[..., 256 + 64 * face_number : 320 + 64 * face_number] for face_number in range(6)
    ]
    padding = jnp.zeros((local_count, halo_count, 64), jnp.float32)
    penalty_terms = []
    for face_number in range(6):
        left_part = halo_left if face_number == 2 else padding
        right_part = halo_right if face_number == 3 else padding
        across = jnp.concatenate([trace_values[face_number ^ 1], left_part, right_part], axis=1)
        exterior_trace = jnp.take(across, table_rows[:, face_number], axis=1)
        penalty_terms.append(
            numerical_flux_penalty(trace_values[face_number], exterior_trace, face_number)
        )
    stacked_traces = jnp.concatenate(penalty_terms, axis=-1)
    surface = jnp.einsum("iel,kl->iek", stacked_traces, table, precision=lax.Precision.HIGHEST)
    return element_scale[None, :, None] * (volume + lift_factor * surface)


def local(state, forcing, jscale, volume_kernel, neighbour, send_left, send_right):
    local_count = state.shape[0]
    instances = local_count * lax.axis_size("tm")
    table = jnp.asarray(face_table())
    outgoing_right = jnp.take(state, send_right, axis=1)
    leftward_outgoing_faces = jnp.take(state, send_left, axis=1)
    arrived_left = shifted(outgoing_right, "space", 1)
    arrived_right = shifted(leftward_outgoing_faces, "space", -1)
    halo_left = select_face(arrived_left, table, 3)
    halo_right = select_face(arrived_right, table, 2)
    spatial = spatial_term(state, jscale, neighbour, halo_left, halo_right, volume_kernel, table)
    owned = lax.axis_index("tm") * local_count + jnp.arange(local_count, dtype=jnp.int32)
    piece = lax.all_gather(state, "tm", axis=0, tiled=True)
    others = jnp.arange(piece.shape[0], dtype=jnp.int32)
    weights = spectral(owned[:, None] - others[None, :], instances)
    deriv = jnp.einsum("nm,mek->nek", weights, piece, precision=lax.Precision.HIGHEST)
    resid = deriv + spatial - forcing
    updated_state = state - (step_factor / jscale)[None, :, None] * resid
    return (resid, updated_state)


def solution(mesh):
    in_specs = (
        P("tm", "space", None),
        P("tm", "space", None),
        P("space"),
        P(),
        P("space", None),
        P("space"),
        P("space"),
    )
    out_specs = (P("tm", "space", None), P("tm", "space", None))
    return jax.shard_map(local, mesh=mesh, in_specs=in_specs, out_specs=out_specs, check_vma=False)
```

profile of v0, /device:TPU:0, one launch (start us, length us, event | category | flops | bytes accessed | tf_op | source)
XLA Modules:
  0.0 88.1 jit_solution(7929773050556520845)
XLA Ops:
  7.2 0.0 all-gather.2.cloned.1.call-start
  7.2 0.7 all-gather.2.cloned.1.call-update
  7.9 0.7 compare_select_fusion.7
  8.6 0.7 compare_and_fusion.5
  9.3 1.9 %gather_fusion.2 = f32[64,2,256]{2,0,1:T(8,128)S(1)} fusion(f32[2,256,256]{2,1,0:T(8,128)} %param.12, s32[1024]{0:T(1024)S(1)} %pad_clamp_fusion.5), kind=kCustom, calls=%fused_computation.1.clone | custom fusion | bytes 262400 | tf_op jit(solution)/shard_map/jit(_take)/gather | solution.py:90
  11.1 0.1 select_bitcast_fusion.1
  11.2 3.1 %collective-permute-start = (f32[2,64,256]{2,1,0:T(8,128)S(1)}, f32[2,64,256]{2,1,0:T(8,128)}, u32[]{:S(2)}, u32[]{:S(2)}) collective-permute-start(f32[2,64,256]{2,1,0:T(8,128)S(1)} %select_bitcast_fusion.1), channel_id=1, source_target_pairs={{3,0},{0,1},{1,2},{2,3},{7,4},{4,5},{5,6},{6,7},{11,8},{8,9},{9,10... | collective-permute-start | bytes 393224 | tf_op jit(solution)/shard_map/ppermute | solution.py:14
  14.3 0.8 gather_fusion.4
  15.1 0.7 select_bitcast_fusion
  15.8 2.1 %collective-permute-start.1 = (f32[2,64,256]{2,1,0:T(8,128)}, f32[2,64,256]{2,1,0:T(8,128)}, u32[]{:S(2)}, u32[]{:S(2)}) collective-permute-start(f32[2,64,256]{2,1,0:T(8,128)} %select_bitcast_fusion), channel_id=1, source_target_pairs={{1,0},{2,1},{3,2},{0,3},{5,4},{6,5},{7,6},{4,7},{9,8},{10,9},{11,1... | collective-permute-start | bytes 393224 | tf_op jit(solution)/shard_map/ppermute | solution.py:14
  17.9 0.1 copy.35
  18.0 1.2 %fusion.10 = f32[640,2,256]{2,0,1:T(8,128)S(1)} fusion(f32[2,256,256]{2,1,0:T(8,128)S(1)} %copy-done, f32[256,384]{0,1:T(8,128)S(1)} %copy-done.4, f32[256,256]{0,1:T(8,128)S(1)} %copy.35), kind=kOutput, calls=%fused_computation.15 | convolution fusion | flops 1006796800 | bytes 2490368 | tf_op jit(solution)/shard_map/iek,kl->iel/dot_general | solution.py:66
  19.3 1.4 %copy.36 = f32[640,2,256]{0,1,2:T(2,128)S(1)} copy(f32[640,2,256]{2,0,1:T(8,128)S(1)} %fusion.10) | data formatting | bytes 2621440 | tf_op jit(solution)/shard_map/iek,kl->iel/dot_general | solution.py:66
  20.9 0.6 pad_clamp_fusion.6
  21.5 0.5 compare_and_fusion
  22.0 0.6 compare_and_fusion.1
  22.5 0.5 compare_and_fusion.4
  23.1 0.5 compare_and_fusion.6
  23.6 0.5 compare_and_fusion.7
  24.1 0.6 compare_and_fusion.2
  24.7 0.6 compare_select_fusion.2
  25.3 0.6 broadcast_divide_fusion
  25.9 1.9 %fusion.52 = (f32[2,256,64]{2,0,1:T(2,128)S(1)}, f32[2,256,64]{2,0,1:T(2,128)S(1)}, f32[2,256,64]{2,0,1:T(2,128)}, f32[2,256,64]{2,0,1:T(2,128)}, f32[2,256,64]{2,0,1:T(2,128)S(1)}, /*index=5*/f32[2,256,64]{2,0,1:T(2,128)S(1)}) fusion(f32[2,256,640]{2,0,1:T(2,128)S(1)} %bitcast.40), kind=kLoop, calls=%fused_computation.119 | loop fusion | bytes 1572864 | tf_op jit(solution)/shard_map/slice | solution.py:69
  27.7 0.5 iota_add_fusion
  28.2 0.1 concatenate.29
  28.3 0.1 concatenate.30
  28.4 0.1 concatenate.25
  28.6 0.1 concatenate.26
  28.7 1.7 %gather_fusion.6 = f32[256,2,64]{2,1,0:T(2,128)} fusion(f32[2,384,64]{2,0,1:T(2,128)S(1)} %concatenate.29, s32[1024]{0:T(1024)S(1)} %pad_clamp_fusion.1), kind=kCustom, calls=%fused_computation.5.clone | custom fusion | bytes 263168 | tf_op jit(solution)/shard_map/jit(_take)/gather | solution.py:77
  30.4 1.7 %gather_fusion.7 = f32[256,2,64]{2,1,0:T(2,128)} fusion(f32[2,384,64]{2,0,1:T(2,128)S(1)} %concatenate.30, s32[1024]{0:T(1024)S(1)} %pad_clamp_fusion), kind=kCustom, calls=%fused_computation.6.clone | custom fusion | bytes 263168 | tf_op jit(solution)/shard_map/jit(_take)/gather | solution.py:77
  32.0 1.7 %gather_fusion = f32[256,2,64]{2,1,0:T(2,128)} fusion(f32[2,384,64]{2,0,1:T(2,128)S(1)} %concatenate.25, s32[1024]{0:T(1024)S(1)} %pad_clamp_fusion.7), kind=kCustom, calls=%fused_computation.clone | custom fusion | bytes 263168 | tf_op jit(solution)/shard_map/jit(_take)/gather | solution.py:77
  33.7 1.8 %gather_fusion.1 = f32[256,2,64]{2,1,0:T(2,128)} fusion(f32[2,384,64]{2,0,1:T(2,128)S(1)} %concatenate.26, s32[1024]{0:T(1024)} %pad_clamp_fusion.6), kind=kCustom, calls=%fused_computation.2.clone | custom fusion | bytes 263168 | tf_op jit(solution)/shard_map/jit(_take)/gather | solution.py:77
  35.5 1.2 %fusion.54 = f32[2,64,64]{1,2,0:T(8,128)S(1)} fusion(f32[2,64,256]{2,1,0:T(8,128)} %collective-permute-done, f32[256,64,1]{0,1,2:T(8,128)S(1)} %copy-done.7), kind=kOutput, calls=%fused_computation.121 | convolution fusion | flops 25165824 | bytes 229376 | tf_op jit(solution)/shard_map/iek,kl->iel/dot_general | solution.py:47
  36.8 0.1 copy.37
  36.9 1.2 %fusion.55 = f32[2,64,64]{1,2,0:T(8,128)S(1)} fusion(f32[2,64,256]{2,1,0:T(8,128)} %collective-permute-done.1, f32[256,64,1]{0,1,2:T(8,128)S(1)} %copy-done.6), kind=kOutput, calls=%fused_computation.122 | convolution fusion | flops 25165824 | bytes 229376 | tf_op jit(solution)/shard_map/iek,kl->iel/dot_general | solution.py:47
  38.1 0.1 copy.38
  38.3 1.5 %pad_maximum_fusion.1 = (f32[2,384,64]{2,0,1:T(2,128)S(1)}, f32[2,384,64]{2,0,1:T(2,128)S(1)}) fusion(f32[2,64,64]{2,0,1:T(2,128)S(1)} %copy.38, f32[2,64,64]{2,0,1:T(2,128)S(1)} %broadcast_in_dim.31, f32[2,256,64]{2,0,1:T(2,128)} %get-tuple-element.18, f32[2,64,64]{2,0,1:T(2,128)S(1)} %copy.37, f32[2,256,64]{2,0,1:T(2,128)} %get-tuple-element.19), kind=kLoop, calls=%fused_computation.23 | loop fusion | flops 196608 | bytes 753664 | tf_op jit(solution)/shard_map/concatenate | solution.py:76
  39.8 1.7 %gather_fusion.3 = f32[256,2,64]{2,1,0:T(2,128)} fusion(f32[2,384,64]{2,0,1:T(2,128)S(1)} %get-tuple-element.44, s32[1024]{0:T(1024)S(1)} %pad_clamp_fusion.4), kind=kCustom, calls=%fused_computation.3.clone | custom fusion | bytes 263168 | tf_op jit(solution)/shard_map/jit(_take)/gather | solution.py:77
  41.5 1.0 %gather_fusion.5 = f32[256,2,64]{2,1,0:T(2,128)S(1)} fusion(f32[2,384,64]{2,0,1:T(2,128)S(1)} %get-tuple-element.43, s32[1024]{0:T(1024)S(1)} %pad_clamp_fusion.2), kind=kCustom, calls=%fused_computation.4.clone | custom fusion | bytes 263168 | tf_op jit(solution)/shard_map/jit(_take)/gather | solution.py:77
  42.5 5.4 %bitcast_subtract_fusion = (f32[2,256,64]{2,0,1:T(2,128)S(1)}, f32[2,256,64]{2,0,1:T(2,128)S(1)}, f32[2,256,64]{2,0,1:T(2,128)S(1)}, f32[2,256,64]{2,0,1:T(2,128...) fusion(f32[256,2,64]{2,1,0:T(2,128)S(1)} %copy-done.2, pred[256]{0:T(512)(128)(4,1)S(1)} %copy-done.14, ...), kind=kLoop, calls=%fused_computation.42 | loop fusion | flops 393216 | bytes 2360832 | tf_op jit(solution)/shard_map/sub | solution.py:51
  47.9 2.9 %slice_multiply_fusion.2 = (f32[2,256,16]{2,0,1:T(2,128)}, f32[2,256,16]{2,0,1:T(2,128)}, f32[2,256,16]{2,0,1:T(2,128)S(1)}, f32[2,256,16]{2,0,1:T(2,128)}, f32[...) fusion(f32[2,256,64]{2,0,1:T(2,128)S(1)} %get-tuple-element.15, ...), kind=kLoop, calls=%fused_computation.26 | loop fusion | flops 98304 | bytes 491520 | tf_op jit(solution)/shard_map/mul | solution.py:54
  50.8 2.9 %slice_multiply_fusion.6 = (f32[2,256,16]{2,0,1:T(2,128)}, f32[2,256,16]{2,0,1:T(2,128)}, f32[2,256,16]{2,0,1:T(2,128)S(1)}, f32[2,256,16]{2,0,1:T(2,128)}, f32[...) fusion(f32[2,256,64]{2,0,1:T(2,128)S(1)} %get-tuple-element.14, ...), kind=kLoop, calls=%fused_computation.32 | loop fusion | flops 98304 | bytes 491520 | tf_op jit(solution)/shard_map/mul | solution.py:54
  53.7 2.8 %slice_multiply_fusion.10 = (f32[2,256,16]{2,0,1:T(2,128)}, f32[2,256,16]{2,0,1:T(2,128)}, f32[2,256,16]{2,0,1:T(2,128)S(1)}, f32[2,256,16]{2,0,1:T(2,128)}, f32...) fusion(f32[2,256,64]{2,0,1:T(2,128)S(1)} %get-tuple-element.12, ...), kind=kLoop, calls=%fused_computation.38 | loop fusion | flops 98304 | bytes 491520 | tf_op jit(solution)/shard_map/mul | solution.py:54
  56.5 13.2 %concatenate.31 = f32[2,256,384]{2,0,1:T(2,128)S(1)} concatenate(f32[2,256,16]{2,0,1:T(2,128)S(1)} %get-tuple-element.42, f32[2,256,16]{2,0,1:T(2,128)S(1)} %get-tuple-element.42, f32[2,256,16]{2,0,1:T(2,128)} %get-tuple-element.41, f32[2,256,16]{2,0,1:T(2,128)} %get-tuple-element.40, f32[2,256,16]{2,0,1:T(2,128)} %get-tuple-element.58, f32[2,256,16]{2,0,1:T(2,128)} %get-tuple-element.57, ...), dimensions={2} | concatenate | bytes 1572864 | tf_op jit(solution)/shard_map/concatenate | solution.py:81
  69.7 2.0 %fusion.8 = f32[2,256,256]{2,1,0:T(8,128)S(1)} fusion(f32[256,384,1]{0,1,2:T(8,128)} %constant.81, f32[2,256,384]{2,0,1:T(2,128)S(1)} %concatenate.31), kind=kOutput, calls=%fused_computation.12 | convolution fusion | flops 603979776 | bytes 1703936 | tf_op jit(solution)/shard_map/iel,kl->iek/dot_general | solution.py:82
  71.7 7.8 %copy_subtract_fusion = (f32[2,256,256]{2,0,1:T(2,128)S(1)}, f32[2,256,256]{2,0,1:T(2,128)S(1)}) fusion(f32[2,256,256]{2,1,0:T(8,128)S(1)} %copy-done, f32[256]{0:T(256)S(1)} %copy-done.11, f32[2,256,256]{2,1,0:T(8,128)} %param.13, f32[2,256,256]{2,1,0:T(8,128)S(1)} %fusion.8, f32[2,256,640]{2,0,1:T(2,128)S(1)} %bitcast.42, f32[256]{0:T(256)S(1)} %copy-done.10, ...), kind=kOutput, calls=%fused_computation.20 | convolution fusion | flops 26084064 | bytes 7342088 | tf_op jit(solution)/shard_map/nm,mek->nek/dot_general | solution.py:101
  79.5 0.8 copy.44
  80.4 0.8 copy.45
  (53 shorter events, 0.2 us)
Async XLA Ops:
  7.2 7.2 %copy-start = (f32[2,256,256]{2,1,0:T(8,128)S(1)}, f32[2,256,256]{2,1,0:T(8,128)}, u32[]{:S(2)}) copy-start(f32[2,256,256]{2,1,0:T(8,128)} %param.12) | copy-start | bytes 1572868
  7.2 7.1 %copy-start.16 = (s32[64]{0:T(128)S(1)}, s32[64]{0:T(128)}, u32[]{:S(2)}) copy-start(s32[64]{0:T(128)} %param.17) | copy-start | bytes 772
  7.2 64.5 %all-gather.2.cloned.1.call-start = ((), (), s32[]{:S(2)}) async-start(), calls=%async_computation | async-start | bytes 4718592 | tf_op jit(solution)/shard_map/all_gather | solution.py:98
  9.2 8.7 %copy-start.5 = (f32[256,256]{1,0:T(8,128)S(1)}, f32[256,256]{1,0:T(8,128)}, u32[]{:S(2)}) copy-start(f32[256,256]{1,0:T(8,128)} %param.15) | copy-start | bytes 786436
  11.1 6.9 %copy-start.4 = (f32[256,384]{0,1:T(8,128)S(1)}, f32[256,384]{0,1:T(8,128)}, u32[]{:S(2)}) copy-start(f32[256,384]{0,1:T(8,128)} %constant.66.clone) | copy-start | bytes 1179652
  11.2 24.3 %collective-permute-start = (f32[2,64,256]{2,1,0:T(8,128)S(1)}, f32[2,64,256]{2,1,0:T(8,128)}, u32[]{:S(2)}, u32[]{:S(2)}) collective-permute-start(f32[2,64,256]{2,1,0:T(8,128)S(1)} %select_bitcast_fusion.1), channel_id=1, source_target_pairs={{3,0},{0,1},{1,2},{2,3},{7,4},{4,5},{5,6},{6,7},{11,8},{8,9},{9,10... | collective-permute-start | bytes 393224 | tf_op jit(solution)/shard_map/ppermute | solution.py:14
  15.8 21.0 %collective-permute-start.1 = (f32[2,64,256]{2,1,0:T(8,128)}, f32[2,64,256]{2,1,0:T(8,128)}, u32[]{:S(2)}, u32[]{:S(2)}) collective-permute-start(f32[2,64,256]{2,1,0:T(8,128)} %select_bitcast_fusion), channel_id=1, source_target_pairs={{1,0},{2,1},{3,2},{0,3},{5,4},{6,5},{7,6},{4,7},{9,8},{10,9},{11,1... | collective-permute-start | bytes 393224 | tf_op jit(solution)/shard_map/ppermute | solution.py:14
  19.3 1.4 %copy-start.8 = (s32[256,6]{0,1:T(8,128)S(1)}, s32[256,6]{0,1:T(8,128)}, u32[]{:S(2)}) copy-start(s32[256,6]{0,1:T(8,128)} %param.16) | copy-start | bytes 18436
  19.3 6.0 %copy-start.9 = (f32[256]{0:T(256)S(1)}, f32[256]{0:T(256)}, u32[]{:S(2)}) copy-start(f32[256]{0:T(256)} %param.14) | copy-start | bytes 3076
  30.4 5.1 %copy-start.12 = (s32[256]{0:T(256)S(1)}, s32[256]{0:T(256)}, u32[]{:S(2)}) copy-start(s32[256]{0:T(256)} %compare_select_fusion.2) | copy-start | bytes 3076
  30.4 5.2 %copy-start.7 = (f32[256,64,1]{0,1,2:T(8,128)S(1)}, f32[256,64,1]{0,1,2:T(8,128)}, u32[]{:S(2)}) copy-start(f32[256,64,1]{0,1,2:T(8,128)} %constant.79) | copy-start | bytes 196612
  30.4 6.5 %copy-start.6 = (f32[256,64,1]{0,1,2:T(8,128)S(1)}, f32[256,64,1]{0,1,2:T(8,128)}, u32[]{:S(2)}) copy-start(f32[256,64,1]{0,1,2:T(8,128)} %constant.80) | copy-start | bytes 196612
  38.2 4.2 %copy-start.1 = (f32[256,2,64]{2,1,0:T(2,128)S(1)}, f32[256,2,64]{2,1,0:T(2,128)}, u32[]{:S(2)}) copy-start(f32[256,2,64]{2,1,0:T(2,128)} %gather_fusion.6) | copy-start | bytes 393220
  38.2 4.2 %copy-start.2 = (f32[256,2,64]{2,1,0:T(2,128)S(1)}, f32[256,2,64]{2,1,0:T(2,128)}, u32[]{:S(2)}) copy-start(f32[256,2,64]{2,1,0:T(2,128)} %gather_fusion.7) | copy-start | bytes 393220
  38.2 4.2 %copy-start.3 = (f32[256,2,64]{2,1,0:T(2,128)S(1)}, f32[256,2,64]{2,1,0:T(2,128)}, u32[]{:S(2)}) copy-start(f32[256,2,64]{2,1,0:T(2,128)} %gather_fusion) | copy-start | bytes 393220
  38.2 4.2 %copy-start.14 = (pred[256]{0:T(512)(128)(4,1)S(1)}, pred[256]{0:T(512)(128)(4,1)}, u32[]{:S(2)}) copy-start(pred[256]{0:T(512)(128)(4,1)} %compare_and_fusion) | copy-start | bytes 772
  38.2 4.2 %copy-start.15 = (pred[256]{0:T(512)(128)(4,1)S(1)}, pred[256]{0:T(512)(128)(4,1)}, u32[]{:S(2)}) copy-start(pred[256]{0:T(512)(128)(4,1)} %compare_and_fusion.1) | copy-start | bytes 772
  69.6 2.1 %copy-start.10 = (f32[256]{0:T(256)S(1)}, f32[256]{0:T(256)}, u32[]{:S(2)}) copy-start(f32[256]{0:T(256)} %param.14) | copy-start | bytes 3076
  69.6 2.1 %copy-start.11 = (f32[256]{0:T(256)S(1)}, f32[256]{0:T(256)}, u32[]{:S(2)}) copy-start(f32[256]{0:T(256)} %broadcast_divide_fusion) | copy-start | bytes 3076
  69.6 2.1 %copy-start.13 = (s32[2]{0:T(128)S(1)}, s32[2]{0:T(128)}, u32[]{:S(2)}) copy-start(s32[2]{0:T(128)} %iota_add_fusion) | copy-start | bytes 28
Sparse Core Ops, SparseCore 0:
  9.9 39.4 all-gather.1
where the time goes:
time: 89.6 us; the launch traced here: 88.1 us
  local copies, waits for them, and re-layouts  31 us (35%)
  other arithmetic  23.2 us (26%)
  between operations  14.5 us (16%)
  matrix products  13.5 us (15%)
  starting transfers between devices  5.17 us (6%)
    concatenate x1, local copies, waits for them, and re-layouts, spatial_term(): stacked_traces = jnp.concatenate(penalty_terms, axis=-1)  13.2 us
    gather x6, local copies, waits for them, and re-layouts, spatial_term(): exterior_trace = jnp.take(across, table_rows[:, face_number], axis=1)  9.44 us
    mul x3, other arithmetic, numerical_flux_penalty(): -0.5 * jump_value[..., 16 * comp_id:16 * comp_id + 16]  8.54 us
    dot_general x1, matrix products, local(): jnp.einsum('nm,mek->nek', weights, piece, precision=lax.Precision.HIGHEST)  7.83 us
    sub x1, other arithmetic, numerical_flux_penalty(): jump_value = exterior_trace - minus  5.41 us
    ppermute x2, starting transfers between devices, shifted(): return lax.ppermute(block, axis, route)  5.14 us
    and x6, other arithmetic, spatial_term(): exterior_trace = jnp.take(across, table_rows[:, face_number], axis=1)  3.23 us
    dot_general x2, matrix products, select_face(): jnp.einsum('iek,kl->iel', blocks, columns, precision=lax.Precision.HIGHEST)  2.45 us
  transfers between devices with their start and end apart: 3, of which 0 were waited for; matrix products, arithmetic and copies ran while one was open for 66% of the time, Pallas kernels for 0%

commit v1 on v0

v1 whole, which is shorter than its diff:
```python
import functools

import jax
import jax.numpy as jnp
import numpy as np
from jax import lax
from jax.experimental import pallas as pl
from jax.experimental.pallas import tpu as pltpu
from jax.sharding import PartitionSpec as P

lift_factor = 2.0
step_factor = 0.2
CELLS = 256
HALO = 64
MESH = pl.DeviceIdType.MESH
F32, BF16 = jnp.float32, jnp.bfloat16


def face_nodes(face):
    end, axis = (3 if face % 2 else 0), face // 2
    cube = np.arange(64).reshape(4, 4, 4)
    return np.take(cube, end, axis=axis).reshape(-1)


def flux_table(source_face, face):
    source, target = face_nodes(source_face), face_nodes(face)
    sign, axis = (1.0 if face % 2 else -1.0), face // 2
    mix = -np.eye(4)
    mix[1 + axis, 0] += sign
    mix[0, 1 + axis] += sign
    table = np.zeros((4, 64, 4, 64))
    for a in range(16):
        table[:, source[a], :, target[a]] = 0.5 * lift_factor * mix
    return table.reshape(256, 256)


def lag_table(instances):
    lag = np.arange(-(instances - 1), instances)
    angle = np.pi * lag / instances
    sine = np.where(lag == 0, 1.0, np.sin(angle))
    value = 0.5 * (1.0 - 2.0 * (lag % 2)) * np.cos(angle) / sine
    return np.where(lag == 0, 0.0, value).astype(np.float32)


def halves(value):
    high = value.astype(BF16)
    return high, (value - high.astype(F32)).astype(BF16)


def dot(a, b):
    return jnp.dot(a, b, preferred_element_type=F32)


def kernel(sizes, lags, state, volume_kernel, minus, plus, neighbour, jscale, send_left, send_right, out,
           pack, split, acc, give, halo, g0, g1, p0, p1, r0, r1,
           hs, hr, s10, q10, s11, q11, s20, q20, s21, q21):
    xs, ys, zs = sizes
    local, count, _ = state.shape
    quarter = count // 4
    instances = local * 2 * xs * ys
    t, z = lax.axis_index("tm"), lax.axis_index("space")
    core, chip = lax.rem(t, 2), lax.div(t, 2)
    x, y = lax.rem(chip, xs), lax.div(chip, xs)
    up, down = lax.rem(z + 1, zs), lax.rem(z + zs - 1, zs)

    def at(yy, xx, cc):
        return {"tm": (yy * xs + xx) * 2 + cc, "space": z}

    def turn(base, step, size):
        return lax.rem(base + step, size) if step else base

    def other(cc, step):
        return 1 - cc if step else cc

    row = [(dx, dc) for dx in range(xs) for dc in range(2)]
    column = [(dy, dc) for dy in range(ys) for dc in range(2)]
    peers = [at(y, turn(x, dx, xs), other(core, dc)) for dx, dc in row[1:]]
    peers += [at(turn(y, dy, ys), x, other(core, dc)) for dy, dc in column if dy]
    peers += [{"tm": t, "space": up}, {"tm": t, "space": down}]
    barrier = pltpu.get_barrier_semaphore()
    for peer in peers:
        pl.semaphore_signal(barrier, inc=1, device_id=peer, device_id_type=MESH)
    pl.semaphore_wait(barrier, len(peers))

    def rows(half, cc):
        return pl.ds(pl.multiple_of((2 * half + cc) * quarter, quarter), quarter)

    plans = (
        (row, column, x, y, xs, ys, g0, p0, r0, s10, q10, s20, q20),
        (column, row, y, x, ys, xs, g1, p1, r1, s11, q11, s21, q21),
    )

    def target(half, first, second, cc):
        return at(second, first, cc) if half == 0 else at(first, second, cc)

    def first_copy(half, step, sending):
        (along, _, me, fixed, size, _, g, _, _, s, q, _, _), (d, dc) = plans[half], step
        mate, mate_core = turn(me, d, size), other(core, dc)
        slot = (me, core) if sending else (mate, mate_core)
        return pltpu.make_async_remote_copy(
            src_ref=state.at[:, rows(half, mate_core)], dst_ref=g.at[slot],
            send_sem=s.at[mate, mate_core], recv_sem=q.at[slot],
            device_id=target(half, mate, fixed, mate_core), device_id_type=MESH)

    def second_copy(half, step, sending):
        (_, _, fixed, me, _, size, _, p, r, _, _, s, q), (d, dc) = plans[half], step
        mate, mate_core = turn(me, d, size), other(core, dc)
        slot = (core, me) if sending else (mate_core, mate)
        return pltpu.make_async_remote_copy(
            src_ref=p.at[mate, mate_core], dst_ref=r.at[slot],
            send_sem=s.at[mate, mate_core], recv_sem=q.at[slot],
            device_id=target(half, fixed, mate, mate_core), device_id_type=MESH)

    firsts = [(half, step) for half in (0, 1) for step in plans[half][0] if step[0]]
    firsts += [(half, (0, 1)) for half in (0, 1)]
    for half, step in firsts:
        first_copy(half, step, True).start()

    pack[0:6, :] = neighbour[...].astype(F32)
    pack[6:7, :] = jscale[...]
    pack[7:8, 0:HALO] = send_left[...].astype(F32)
    pack[7:8, HALO:2 * HALO] = send_right[...].astype(F32)
    pack[7:8, 2 * HALO:] = jnp.zeros((1, count - 2 * HALO), F32)
    columns = jnp.transpose(pack[...])
    numbers = columns.astype(jnp.int32)
    scale = columns[:, 6:7]

    for i in range(local):
        high, low = halves(state[i])
        split[:, 2 * i * CELLS:(2 * i + 1) * CELLS] = high
        split[:, (2 * i + 1) * CELLS:(2 * i + 2) * CELLS] = low

    listed = numbers[0:2 * HALO, 7:8]
    chosen = (listed == lax.broadcasted_iota(jnp.int32, (2 * HALO, count), 1)).astype(F32).astype(BF16)
    sent = dot(chosen, split[...])
    for i in range(local):
        value = sent[:, 2 * i * CELLS:(2 * i + 1) * CELLS] + sent[:, (2 * i + 1) * CELLS:(2 * i + 2) * CELLS]
        give[0, i] = value[0:HALO]
        give[1, i] = value[HALO:]

    def halo_copy(side):
        return pltpu.make_async_remote_copy(
            src_ref=give.at[side], dst_ref=halo.at[1 - side], send_sem=hs.at[side], recv_sem=hr.at[1 - side],
            device_id={"tm": t, "space": up if side else down}, device_id_type=MESH)

    for side in (0, 1):
        halo_copy(side).start()

    vh, vl = halves(volume_kernel[...] + minus[...])
    for i in range(local):
        high = split[:, 2 * i * CELLS:(2 * i + 1) * CELLS]
        low = split[:, (2 * i + 1) * CELLS:(2 * i + 2) * CELLS]
        acc[i] = dot(high, vh) + dot(low, vh) + dot(high, vl)
    lanes = lax.broadcasted_iota(jnp.int32, (count, count), 1)

    def add_face(face, picked):
        picked = picked.astype(BF16)
        for i in range(local):
            high = picked[:, 2 * i * CELLS:(2 * i + 1) * CELLS]
            low = picked[:, (2 * i + 1) * CELLS:(2 * i + 2) * CELLS]
            acc[i] += dot(high, plus[face]) + dot(low, plus[face])

    for face in range(6):
        hot = (numbers[:, face:face + 1] == lanes).astype(F32).astype(BF16)
        add_face(face, dot(hot, split[...]))

    for half in (0, 1):
        along, across, me, fixed, size, other_size, g, p, r, _, _, _, _ = plans[half]
        for step in along[1:]:
            first_copy(half, step, False).wait_recv()
        mine = rows(half, core)
        start = (2 * half + core) * quarter

        def number(first, second, cc):
            return (((second * xs + first) if half == 0 else (first * xs + second)) * 2 + cc) * local

        origins = [(turn(me, d, size), other(core, dc)) for d, dc in along]
        for d, dc in [step for step in across if step[0]] + [(0, 1), (0, 0)]:
            mate, mate_core = turn(fixed, d, other_size), other(core, dc)
            base = number(me, mate, mate_core)
            weights = [[[lags[base + n - number(first, fixed, cc) - m + instances - 1] for m in range(local)]
                        for first, cc in origins] for n in range(local)]

            def chunk(k, carry, d=d, dc=dc, mate=mate, mate_core=mate_core, weights=weights):
                here = pl.ds(pl.multiple_of(k * 16, 16), 16)
                totals = [None] * local
                for o, (first, cc) in enumerate(origins):
                    for m in range(local):
                        if o == 0:
                            value = state[m, pl.ds(pl.multiple_of(start + k * 16, 16), 16), :]
                        else:
                            value = g[first, cc, m, here, :]
                        for n in range(local):
                            term = weights[n][o][m] * value
                            totals[n] = term if totals[n] is None else totals[n] + term
                for n in range(local):
                    if d == 0 and dc == 0:
                        r[core, fixed, n, here, :] = totals[n]
                    else:
                        p[mate, mate_core, n, here, :] = totals[n]
                return carry

            lax.fori_loop(0, quarter // 16, chunk, 0)
            if (d, dc) != (0, 0):
                second_copy(half, (d, dc), True).start()

    for side, face in ((0, 2), (1, 3)):
        halo_copy(1 - side).wait_recv()
        first = count + side * HALO
        slots = lax.broadcasted_iota(jnp.int32, (count, HALO), 1) + first
        hot = (numbers[:, face:face + 1] == slots).astype(F32).astype(BF16)
        for i in range(local):
            high, low = halves(halo[side, i])
            for part in (high, low):
                acc[i] += dot(dot(hot, part).astype(BF16), plus[face])

    for half in (0, 1):
        across, other_size, r = plans[half][1], plans[half][5], plans[half][8]
        for step in [s for s in across if s != (0, 0)]:
            second_copy(half, step, False).wait_recv()
        for cc in range(2):
            low = (2 * half + cc) * quarter
            for i in range(local):
                total = r[cc, 0, i]
                for slot in range(1, other_size):
                    total = total + r[cc, slot, i]
                out[i, low:low + quarter, :] = total + scale[low:low + quarter] * acc[i, low:low + quarter, :]

    for half, step in firsts:
        first_copy(half, step, True).wait_send()
    for side in (0, 1):
        halo_copy(side).wait_send()
    for half in (0, 1):
        for step in [s for s in plans[half][1] if s != (0, 0)]:
            second_copy(half, step, True).wait_send()


def local_step(sizes, state, forcing, jscale, volume_kernel, neighbour, send_left, send_right):
    xs, ys, _ = sizes
    local, count, cells = state.shape
    quarter = count // 4
    instances = local * 2 * xs * ys
    lags = jnp.asarray(lag_table(instances))
    plus = jnp.asarray(np.stack([flux_table(f ^ 1, f) for f in range(6)]).astype(np.float32), BF16)
    minus = jnp.asarray(-sum(flux_table(f, f) for f in range(6)).astype(np.float32))
    block = (local, quarter, cells)
    sems = pltpu.SemaphoreType.DMA
    vmem = pl.BlockSpec(memory_space=pltpu.VMEM)
    term = pl.pallas_call(
        functools.partial(kernel, sizes),
        out_shape=jax.ShapeDtypeStruct(state.shape, F32),
        in_specs=[pl.BlockSpec(memory_space=pltpu.SMEM)] + [vmem] * 8,
        out_specs=vmem,
        scratch_shapes=[
            pltpu.VMEM((8, count), F32),
            pltpu.VMEM((count, 2 * local * cells), BF16),
            pltpu.VMEM(state.shape, F32),
            pltpu.VMEM((2, local, HALO, cells), F32),
            pltpu.VMEM((2, local, HALO, cells), F32),
            pltpu.VMEM((xs, 2) + block, F32),
            pltpu.VMEM((ys, 2) + block, F32),
            pltpu.VMEM((ys, 2) + block, F32),
            pltpu.VMEM((xs, 2) + block, F32),
            pltpu.VMEM((2, ys) + block, F32),
            pltpu.VMEM((2, xs) + block, F32),
            sems((2,)), sems((2,)),
            sems((xs, 2)), sems((xs, 2)),
            sems((ys, 2)), sems((ys, 2)),
            sems((ys, 2)), sems((2, ys)),
            sems((xs, 2)), sems((2, xs)),
        ],
        compiler_params=pltpu.CompilerParams(
            collective_id=0, has_side_effects=True, vmem_limit_bytes=48 * 2**20),
        cost_estimate=pl.CostEstimate(flops=4 * 10**9, bytes_accessed=4 * 2**20, transcendentals=0),
    )(lags, state, volume_kernel, minus, plus, neighbour.T, jscale.reshape(1, -1),
      send_left.reshape(1, -1), send_right.reshape(1, -1))
    residual = term - forcing
    return residual, state - (step_factor / jscale)[None, :, None] * residual


def solution(mesh):
    chips = mesh.shape["tm"] // 2
    xs = max(d for d in range(1, chips + 1) if chips % d == 0 and d * d <= chips)
    sizes = (xs, chips // xs, mesh.shape["space"])
    field = P("tm", "space", None)
    in_specs = (field, field, P("space"), P(), P("space", None), P("space"), P("space"))
    return jax.shard_map(functools.partial(local_step, sizes), mesh=mesh, in_specs=in_specs,
                         out_specs=(field, field), check_vma=False)
```

time: 89.6 us -> 29.6 us (0.33); the launches traced: 88.1 us -> 29.2 us
  local copies, waits for them, and re-layouts: 31 us -> 6.12 us
  other arithmetic: 23.2 us -> 1.11 us
  Pallas kernels: 0 us -> 21.3 us
  between operations: 14.5 us -> 0.67 us
  matrix products: 13.5 us -> 0 us
  starting transfers between devices: 5.17 us -> 0 us
    pallas_call x0 -> x1, Pallas kernels: none -> 21.3 us  [local_step(): pl.pallas_call(functools.partial(kernel, sizes), out_shape=jax.ShapeDtype...]
    concatenate x5 -> x0, local copies, waits for them, and re-layouts: 13.6 us -> none  [the longest x1 13.2 us: spatial_term(): stacked_traces = jnp.concatenate(penalty_terms, axis=-1)]
    dot_general x5 -> x0, matrix products: 13.5 us -> none  [the longest x1 7.83 us: local(): jnp.einsum('nm,mek->nek', weights, piece, precision=lax.Precision.HIGHEST)]
    gather x8 -> x0, local copies, waits for them, and re-layouts: 12.1 us -> none  [the longest x6 9.44 us: spatial_term(): exterior_trace = jnp.take(across, table_rows[:, face_number], axis=1)]
    mul x3 -> x0, other arithmetic: 8.54 us -> none  [numerical_flux_penalty(): -0.5 * jump_value[..., 16 * comp_id:16 * comp_id + 16]]
    ppermute x2 -> x0, starting transfers between devices: 5.14 us -> none  [shifted(): return lax.ppermute(block, axis, route)]
    sub x1, other arithmetic: 5.41 us -> 1.1 us  [local_step(): return (residual, state - (step_factor / jscale)[None, :, None] * residual)]
    unnamed x37 -> x20, local copies, waits for them, and re-layouts: 1.87 us -> 6.12 us
  transfers between devices with their start and end apart: 3 -> 0, of which waited for: 0 -> 0; matrix products, arithmetic and copies ran while one was open for 66% -> 0% of each run, Pallas kernels for 0% -> 0%
where the time goes in v1:
time: 29.6 us; the launch traced here: 29.2 us
  Pallas kernels  21.3 us (72%)
  local copies, waits for them, and re-layouts  6.12 us (21%)
  other arithmetic  1.11 us (4%)
  between operations  0.67 us (2%)
    pallas_call x1, Pallas kernels, local_step(): pl.pallas_call(functools.partial(kernel, sizes), out_shape=jax.ShapeDtype...  21.3 us
    unnamed x20, local copies, waits for them, and re-layouts  6.12 us
    sub x1, other arithmetic, local_step(): return (residual, state - (step_factor / jscale)[None, :, None] * residual)  1.1 us

profile of v1, /device:TPU:0, one launch (start us, length us, event | category | flops | bytes accessed | tf_op | source)
XLA Modules:
  0.0 29.2 jit_solution(5767149547557823577)
XLA Ops:
  0.6 0.0 copy-start.1
  0.6 0.7 %copy-done.1 = f32[256]{0:T(256)S(1)} copy-done((f32[256]{0:T(256)S(1)}, f32[256]{0:T(256)}, u32[]{:S(2)}) %copy-start.1) | copy-done | bytes 1048
  1.3 0.0 copy-start.4
  1.3 0.0 copy-start.5
  1.3 0.0 copy-start.8
  1.3 0.6 %copy-done.4 = s32[64]{0:T(128)S(1)} copy-done((s32[64]{0:T(128)S(1)}, s32[64]{0:T(128)}, u32[]{:S(2)}) %copy-start.4) | copy-done | bytes 280
  2.0 0.0 copy-done.5
  2.0 0.0 copy-done.8
  2.0 0.0 copy-start
  2.0 1.0 %copy-done = f32[2,256,256]{2,1,0:T(8,128)S(1)} copy-done((f32[2,256,256]{2,1,0:T(8,128)S(1)}, f32[2,256,256]{2,1,0:T(8,128)}, u32[]{:S(2)}) %copy-start) | copy-done | bytes 524312
  3.0 0.0 copy-start.2
  3.0 0.9 %copy-done.2 = f32[256,256]{1,0:T(8,128)S(1)} copy-done((f32[256,256]{1,0:T(8,128)S(1)}, f32[256,256]{1,0:T(8,128)}, u32[]{:S(2)}) %copy-start.2) | copy-done | bytes 262168
  4.0 0.0 copy-start.3
  4.0 0.7 %copy-done.3 = s32[256,6]{0,1:T(8,128)S(1)} copy-done((s32[256,6]{0,1:T(8,128)S(1)}, s32[256,6]{0,1:T(8,128)}, u32[]{:S(2)}) %copy-start.3) | copy-done | bytes 6168
  4.7 0.0 copy-start.6
  4.7 1.1 %copy-done.6 = bf16[6,256,256]{2,1,0:T(8,128)(2,1)S(1)} copy-done((bf16[6,256,256]{2,1,0:T(8,128)(2,1)S(1)}, bf16[6,256,256]{2,1,0:T(8,128)(2,1)}, u32[]{:S(2)}) %copy-start.6) | copy-done | bytes 786456
  5.8 0.0 copy-start.7
  5.8 0.9 %copy-done.7 = f32[256,256]{1,0:T(8,128)S(1)} copy-done((f32[256,256]{1,0:T(8,128)S(1)}, f32[256,256]{1,0:T(8,128)}, u32[]{:S(2)}) %copy-start.7) | copy-done | bytes 262168
  6.8 0.0 copy-start.9
  6.8 21.3 %shard_map.113 = f32[2,256,256]{2,1,0:T(8,128)S(1)} custom-call(f32[31]{0:T(128)S(1)} %copy-done.8, f32[2,256,256]{2,1,0:T(8,128)S(1)} %copy-done, f32[256,256]{1,0:T(8,128)S(1)} %copy-done.2, f32[256,256]{1,0:T(8,128)S(1)} %copy-done.7, bf16[6,256,256]{2,1,0:T(8,128)(2,1)S(1)} %copy-done.6, s32[6,256]{1,0:T(8,128)S(1)} %bitcast.5, f32[1,256]{1,0:T(1,128)S(1)} %bitcast.4, ...), custom_call_target="tpu_custom_call" | custom-call | flops 4000000000 | bytes 4194304 | tf_op jit(solution)/shard_map/pallas_call | solution.py:249
  28.1 0.0 copy-done.9
  28.1 1.1 %multiply_subtract_fusion = (f32[2,256,256]{2,1,0:T(8,128)}, f32[2,256,256]{2,1,0:T(8,128)}) fusion(f32[2,256,256]{2,1,0:T(8,128)S(1)} %copy-done, f32[256]{0:T(256)S(1)} %broadcast_divide_fusion, f32[2,256,256]{2,1,0:T(8,128)S(1)} %shard_map.113, f32[2,256,256]{2,1,0:T(8,128)S(1)} %copy-done.9), kind=kLoop, calls=%fused_computation | loop fusion | flops 393216 | bytes 2622464 | tf_op jit(solution)/shard_map/sub | solution.py:278
  (1 shorter events, 0.0 us)
Async XLA Ops:
  0.6 0.7 %copy-start.1 = (f32[256]{0:T(256)S(1)}, f32[256]{0:T(256)}, u32[]{:S(2)}) copy-start(f32[256]{0:T(256)} %param.12) | copy-start | bytes 3076
  1.3 0.7 %copy-start.4 = (s32[64]{0:T(128)S(1)}, s32[64]{0:T(128)}, u32[]{:S(2)}) copy-start(s32[64]{0:T(128)} %param.15) | copy-start | bytes 772
  1.3 0.7 %copy-start.5 = (s32[64]{0:T(128)S(1)}, s32[64]{0:T(128)}, u32[]{:S(2)}) copy-start(s32[64]{0:T(128)} %param.16) | copy-start | bytes 772
  1.3 0.7 %copy-start.8 = (f32[31]{0:T(128)S(1)}, f32[31]{0:T(128)}, u32[]{:S(2)}) copy-start(f32[31]{0:T(128)} %constant.8.clone.lags) | copy-start | bytes 376
  2.0 1.0 %copy-start = (f32[2,256,256]{2,1,0:T(8,128)S(1)}, f32[2,256,256]{2,1,0:T(8,128)}, u32[]{:S(2)}) copy-start(f32[2,256,256]{2,1,0:T(8,128)} %state.1) | copy-start | bytes 1572868
  3.0 0.9 %copy-start.2 = (f32[256,256]{1,0:T(8,128)S(1)}, f32[256,256]{1,0:T(8,128)}, u32[]{:S(2)}) copy-start(f32[256,256]{1,0:T(8,128)} %volume_kernel.1) | copy-start | bytes 786436
  4.0 0.7 %copy-start.3 = (s32[256,6]{0,1:T(8,128)S(1)}, s32[256,6]{0,1:T(8,128)}, u32[]{:S(2)}) copy-start(s32[256,6]{0,1:T(8,128)} %param.14) | copy-start | bytes 18436
  4.7 1.1 %copy-start.6 = (bf16[6,256,256]{2,1,0:T(8,128)(2,1)S(1)}, bf16[6,256,256]{2,1,0:T(8,128)(2,1)}, u32[]{:S(2)}) copy-start(bf16[6,256,256]{2,1,0:T(8,128)(2,1)} %constant.9.clone.plus) | copy-start | bytes 2359300
  5.8 0.9 %copy-start.7 = (f32[256,256]{1,0:T(8,128)S(1)}, f32[256,256]{1,0:T(8,128)}, u32[]{:S(2)}) copy-start(f32[256,256]{1,0:T(8,128)} %constant.10.clone.minus) | copy-start | bytes 786436
  6.8 21.3 %copy-start.9 = (f32[2,256,256]{2,1,0:T(8,128)S(1)}, f32[2,256,256]{2,1,0:T(8,128)}, u32[]{:S(2)}) copy-start(f32[2,256,256]{2,1,0:T(8,128)} %param.11) | copy-start | bytes 1572868

commit v2 on v1

v2 whole, which is shorter than its diff:
```python
import functools

import jax
import jax.numpy as jnp
import numpy as np
from jax import lax
from jax.experimental import pallas as pl
from jax.experimental.pallas import tpu as pltpu
from jax.sharding import PartitionSpec as P

lift_factor = 2.0
step_factor = 0.2
CELLS = 256
HALO = 64
GROUP = 128
CHUNKS = 2
MESH = pl.DeviceIdType.MESH
F32, BF16 = jnp.float32, jnp.bfloat16


def face_nodes(face):
    end, axis = (3 if face % 2 else 0), face // 2
    cube = np.arange(64).reshape(4, 4, 4)
    return np.take(cube, end, axis=axis).reshape(-1)


def flux_table(source_rows, face):
    target = face_nodes(face)
    sign, axis = (1.0 if face % 2 else -1.0), face // 2
    mix = -np.eye(4)
    mix[1 + axis, 0] += sign
    mix[0, 1 + axis] += sign
    table = np.zeros((256, 4, 64))
    for a in range(16):
        for c in range(4):
            table[source_rows[c, a], :, target[a]] = 0.5 * lift_factor * mix[c]
    return table.reshape(256, 256)


def block_rows(face):
    return np.arange(4)[:, None] * 64 + face_nodes(face)[None, :]


def tables():
    pick = np.zeros((256, 384))
    for face in range(6):
        pick[block_rows(face).reshape(-1), face * 64 + np.arange(64)] = 1.0
    place = np.concatenate([
        flux_table(np.arange(64).reshape(4, 16) + 64 * (1 - f % 2), f)[:GROUP] for f in range(6)])
    minus = -sum(flux_table(block_rows(f), f) for f in range(6))
    return pick, place, minus


def lag_table(instances):
    lag = np.arange(-(instances - 1), instances)
    angle = np.pi * lag / instances
    sine = np.where(lag == 0, 1.0, np.sin(angle))
    value = 0.5 * (1.0 - 2.0 * (lag % 2)) * np.cos(angle) / sine
    return np.where(lag == 0, 0.0, value).astype(np.float32)


def halves(value):
    high = value.astype(BF16)
    return high, (value - high.astype(F32)).astype(BF16)


def dot(a, b):
    return jnp.dot(a, b, preferred_element_type=F32)


def kernel(sizes, lags_hbm, state, volume_hbm, minus_hbm, pick_hbm, place_hbm, neighbour_hbm, jscale_hbm,
           left_hbm, right_hbm, out, pace,
           lags, own, volume_kernel, minus, pick, place, neighbour, jscale, send_left, send_right,
           pack, split, traces, picked, acc, give, halo, g0, g1, p0, p1, r0, r1,
           load, hs, hr, s10, q10, s11, q11, s20, q20, s21, q21):
    xs, ys, zs = sizes
    local, count, _ = own.shape
    sub = g0.shape[4]
    chunks = g0.shape[2]
    quarter = count // 4
    parts = 2 * local
    instances = local * 2 * xs * ys
    t, z = lax.axis_index("tm"), lax.axis_index("space")
    core, chip = lax.rem(t, 2), lax.div(t, 2)
    x, y = lax.rem(chip, xs), lax.div(chip, xs)
    up, down = lax.rem(z + 1, zs), lax.rem(z + zs - 1, zs)

    def at(yy, xx, cc):
        return {"tm": (yy * xs + xx) * 2 + cc, "space": z}

    def turn(base, step, size):
        return lax.rem(base + step, size) if step else base

    def other(cc, step):
        return 1 - cc if step else cc

    row = [(dx, dc) for dx in range(xs) for dc in range(2)]
    column = [(dy, dc) for dy in range(ys) for dc in range(2)]
    peers = [at(y, turn(x, dx, xs), other(core, dc)) for dx, dc in row[1:]]
    peers += [at(turn(y, dy, ys), x, other(core, dc)) for dy, dc in column if dy]
    peers += [{"tm": t, "space": up}, {"tm": t, "space": down}]
    barrier = pltpu.get_barrier_semaphore()
    for peer in peers:
        pl.semaphore_signal(barrier, inc=1, device_id=peer, device_id_type=MESH)

    loads = [pltpu.make_async_copy(a, b, load.at[k]) for k, (a, b) in enumerate((
        (neighbour_hbm, neighbour), (jscale_hbm, jscale), (left_hbm, send_left), (right_hbm, send_right),
        (state, own), (pick_hbm, pick), (lags_hbm, lags), (volume_hbm, volume_kernel), (minus_hbm, minus),
        (place_hbm, place)))]
    for one in loads:
        one.start()
    pl.semaphore_wait(barrier, len(peers))

    def rows(half, cc, k):
        return pl.ds(pl.multiple_of((2 * half + cc) * quarter + k * sub, sub), sub)

    plans = (
        (row, column, x, y, xs, ys, g0, p0, r0, s10, q10, s20, q20),
        (column, row, y, x, ys, xs, g1, p1, r1, s11, q11, s21, q21),
    )

    def target(half, first, second, cc):
        return at(second, first, cc) if half == 0 else at(first, second, cc)

    def first_copy(half, step, k, sending):
        (along, _, me, fixed, size, _, g, _, _, s, q, _, _), (d, dc) = plans[half], step
        mate, mate_core = turn(me, d, size), other(core, dc)
        slot = (me, core, k) if sending else (mate, mate_core, k)
        return pltpu.make_async_remote_copy(
            src_ref=state.at[:, rows(half, mate_core, k)], dst_ref=g.at[slot],
            send_sem=s.at[mate, mate_core, k], recv_sem=q.at[slot],
            device_id=target(half, mate, fixed, mate_core), device_id_type=MESH)

    def second_copy(half, step, k, sending):
        (_, _, fixed, me, _, size, _, p, r, _, _, s, q), (d, dc) = plans[half], step
        mate, mate_core = turn(me, d, size), other(core, dc)
        slot = (core, me, k) if sending else (mate_core, mate, k)
        return pltpu.make_async_remote_copy(
            src_ref=p.at[mate, mate_core, k], dst_ref=r.at[slot],
            send_sem=s.at[mate, mate_core, k], recv_sem=q.at[slot],
            device_id=target(half, fixed, mate, mate_core), device_id_type=MESH)

    firsts = []
    for k in range(chunks):
        firsts += [(half, step, k) for half in (0, 1) for step in plans[half][0] if step[0]]
        firsts += [(half, (0, 1), k) for half in (0, 1)]
    for one in firsts:
        first_copy(*one, True).start()

    for one in loads[:5]:
        one.wait()
    pack[0:6, :] = neighbour[...].astype(F32)
    pack[6:7, :] = jscale[...]
    pace[...] = step_factor / jscale[...]
    pack[7:8, 0:HALO] = send_left[...].astype(F32)
    pack[7:8, HALO:2 * HALO] = send_right[...].astype(F32)
    pack[7:8, 2 * HALO:] = jnp.zeros((1, count - 2 * HALO), F32)
    columns = jnp.transpose(pack[...])
    numbers = columns.astype(jnp.int32)
    scale = columns[:, 6:7]

    def hot(column, first, size, width):
        lanes = lax.broadcasted_iota(jnp.int32, (size, width), 1) + first
        return (column == lanes).astype(F32).astype(BF16)

    for i in range(local):
        high, low = halves(own[i])
        split[2 * i * count:(2 * i + 1) * count, :] = high
        split[(2 * i + 1) * count:(2 * i + 2) * count, :] = low
    loads[5].wait()
    for part in range(parts):
        found = dot(split[part * count:(part + 1) * count, :], pick[...]).astype(BF16)
        for axis in range(3):
            traces[axis, 0:count, part * GROUP:(part + 1) * GROUP] = found[:, axis * GROUP:(axis + 1) * GROUP]

    sent = dot(hot(numbers[0:2 * HALO, 7:8], 0, 2 * HALO, count), traces[1, 0:count, :])
    for i in range(local):
        value = sent[:, 2 * i * GROUP:(2 * i + 1) * GROUP] + sent[:, (2 * i + 1) * GROUP:(2 * i + 2) * GROUP]
        give[0, i] = value[0:HALO]
        give[1, i] = value[HALO:]

    def halo_copy(side):
        return pltpu.make_async_remote_copy(
            src_ref=give.at[side], dst_ref=halo.at[1 - side], send_sem=hs.at[side], recv_sem=hr.at[1 - side],
            device_id={"tm": t, "space": up if side else down}, device_id_type=MESH)

    for side in (0, 1):
        halo_copy(side).start()

    def gather(faces, width):
        for slot, face in enumerate(faces):
            found = dot(hot(numbers[:, face:face + 1], 0, count, width), traces[face // 2, 0:width, :]).astype(BF16)
            for part in range(parts):
                picked[part * count:(part + 1) * count, face * GROUP:(face + 1) * GROUP] = (
                    found[:, part * GROUP:(part + 1) * GROUP])

    def put(first, last, fresh=False):
        used = slice(first * GROUP, last * GROUP)
        for i in range(local):
            total = None if fresh else acc[i]
            for part in (2 * i, 2 * i + 1):
                term = dot(picked[part * count:(part + 1) * count, used], place[used, :])
                total = term if total is None else total + term
            acc[i] = total

    def volume():
        loads[7].wait()
        loads[8].wait()
        vh, vl = halves(volume_kernel[...] + minus[...].astype(F32))
        for i in range(local):
            high = split[2 * i * count:(2 * i + 1) * count, :]
            low = split[(2 * i + 1) * count:(2 * i + 2) * count, :]
            acc[i] = dot(high, vh) + dot(low, vh) + dot(high, vl)

    def partial(half, k):
        along, across, me, fixed, size, other_size, g, p, r, _, _, _, _ = plans[half]
        for step in along[1:]:
            first_copy(half, step, k, False).wait_recv()
        start = (2 * half + core) * quarter + k * sub

        def number(first, second, cc):
            return (((second * xs + first) if half == 0 else (first * xs + second)) * 2 + cc) * local

        origins = [(turn(me, d, size), other(core, dc)) for d, dc in along]
        for d, dc in [step for step in across if step[0]] + [(0, 1), (0, 0)]:
            mate, mate_core = turn(fixed, d, other_size), other(core, dc)
            base = number(me, mate, mate_core)
            weights = [[[lags[base + n - number(first, fixed, cc) - m + instances - 1] for m in range(local)]
                        for first, cc in origins] for n in range(local)]

            def step16(j, carry, d=d, dc=dc, mate=mate, mate_core=mate_core, weights=weights):
                here = pl.ds(pl.multiple_of(j * 16, 16), 16)
                totals = [None] * local
                for o, (first, cc) in enumerate(origins):
                    for m in range(local):
                        if o == 0:
                            value = own[m, pl.ds(pl.multiple_of(start + j * 16, 16), 16), :]
                        else:
                            value = g[first, cc, k, m, here, :]
                        for n in range(local):
                            term = weights[n][o][m] * value
                            totals[n] = term if totals[n] is None else totals[n] + term
                for n in range(local):
                    if d == 0 and dc == 0:
                        r[core, fixed, k, n, here, :] = totals[n]
                    else:
                        p[mate, mate_core, k, n, here, :] = totals[n]
                return carry

            lax.fori_loop(0, sub // 16, step16, 0)
            if (d, dc) != (0, 0):
                second_copy(half, (d, dc), k, True).start()

    volume()
    gather((0, 1), count)
    loads[6].wait()
    for k in range(chunks):
        for half in (0, 1):
            partial(half, k)
        if k == 0:
            gather((4, 5), count)
    loads[9].wait()
    put(0, 2)
    put(4, 6)

    for side in (0, 1):
        halo_copy(1 - side).wait_recv()
        first = count + side * HALO
        for i in range(local):
            high, low = halves(halo[side, i])
            traces[1, first:first + HALO, 2 * i * GROUP:(2 * i + 1) * GROUP] = high
            traces[1, first:first + HALO, (2 * i + 1) * GROUP:(2 * i + 2) * GROUP] = low
    gather((2, 3), count + 2 * HALO)
    put(2, 4)

    for k in range(chunks):
        for half in (0, 1):
            across, other_size, r = plans[half][1], plans[half][5], plans[half][8]
            for step in [s for s in across if s != (0, 0)]:
                second_copy(half, step, k, False).wait_recv()
            for cc in range(2):
                low = (2 * half + cc) * quarter + k * sub
                for i in range(local):
                    total = r[cc, 0, k, i]
                    for slot in range(1, other_size):
                        total = total + r[cc, slot, k, i]
                    out[i, low:low + sub, :] = total + scale[low:low + sub] * acc[i, low:low + sub, :]

    for one in firsts:
        first_copy(*one, True).wait_send()
    for side in (0, 1):
        halo_copy(side).wait_send()
    for k in range(chunks):
        for half in (0, 1):
            for step in [s for s in plans[half][1] if s != (0, 0)]:
                second_copy(half, step, k, True).wait_send()


def local_step(sizes, state, forcing, jscale, volume_kernel, neighbour, send_left, send_right):
    xs, ys, _ = sizes
    local, count, cells = state.shape
    quarter = count // 4
    sub = quarter // CHUNKS
    instances = local * 2 * xs * ys
    lags = jnp.asarray(lag_table(instances))
    pick, place, minus = [jnp.asarray(table.astype(np.float32), BF16) for table in tables()]
    block = (CHUNKS, local, sub, cells)
    sems = pltpu.SemaphoreType.DMA
    term, pace = pl.pallas_call(
        functools.partial(kernel, sizes),
        out_shape=(jax.ShapeDtypeStruct(state.shape, F32), jax.ShapeDtypeStruct((1, count), F32)),
        in_specs=[pl.BlockSpec(memory_space=pltpu.HBM)] * 10,
        out_specs=[pl.BlockSpec(memory_space=pltpu.VMEM)] * 2,
        scratch_shapes=[
            pltpu.SMEM(lags.shape, F32),
            pltpu.VMEM(state.shape, F32),
            pltpu.VMEM((cells, cells), F32),
            pltpu.VMEM(minus.shape, BF16),
            pltpu.VMEM(pick.shape, BF16),
            pltpu.VMEM(place.shape, BF16),
            pltpu.VMEM((6, count), jnp.int32),
            pltpu.VMEM((1, count), F32),
            pltpu.VMEM((1, HALO), jnp.int32),
            pltpu.VMEM((1, HALO), jnp.int32),
            pltpu.VMEM((8, count), F32),
            pltpu.VMEM((2 * local * count, cells), BF16),
            pltpu.VMEM((3, count + 2 * HALO, 2 * local * GROUP), BF16),
            pltpu.VMEM((2 * local * count, 6 * GROUP), BF16),
            pltpu.VMEM(state.shape, F32),
            pltpu.VMEM((2, local, HALO, GROUP), F32),
            pltpu.VMEM((2, local, HALO, GROUP), F32),
            pltpu.VMEM((xs, 2) + block, F32),
            pltpu.VMEM((ys, 2) + block, F32),
            pltpu.VMEM((ys, 2) + block, F32),
            pltpu.VMEM((xs, 2) + block, F32),
            pltpu.VMEM((2, ys) + block, F32),
            pltpu.VMEM((2, xs) + block, F32),
            sems((10,)), sems((2,)), sems((2,)),
            sems((xs, 2, CHUNKS)), sems((xs, 2, CHUNKS)),
            sems((ys, 2, CHUNKS)), sems((ys, 2, CHUNKS)),
            sems((ys, 2, CHUNKS)), sems((2, ys, CHUNKS)),
            sems((xs, 2, CHUNKS)), sems((2, xs, CHUNKS)),
        ],
        compiler_params=pltpu.CompilerParams(
            collective_id=0, has_side_effects=True, vmem_limit_bytes=60 * 2**20),
        cost_estimate=pl.CostEstimate(flops=3 * 10**9, bytes_accessed=4 * 2**20, transcendentals=0),
    )(lags, state, volume_kernel, minus, pick, place, neighbour.T, jscale.reshape(1, -1),
      send_left.reshape(1, -1), send_right.reshape(1, -1))
    residual = term - forcing
    return residual, state - pace.reshape(1, -1, 1) * residual


def solution(mesh):
    chips = mesh.shape["tm"] // 2
    xs = max(d for d in range(1, chips + 1) if chips % d == 0 and d * d <= chips)
    sizes = (xs, chips // xs, mesh.shape["space"])
    field = P("tm", "space", None)
    in_specs = (field, field, P("space"), P(), P("space", None), P("space"), P("space"))
    return jax.shard_map(functools.partial(local_step, sizes), mesh=mesh, in_specs=in_specs,
                         out_specs=(field, field), check_vma=False)
```

time: 29.6 us -> 23.9 us (0.81)
  local copies, waits for them, and re-layouts: 6.12 us -> 0.64 us
  Pallas kernels: 21.3 us -> 20.2 us
  other arithmetic: 1.11 us -> 2.12 us
    unnamed x20 -> x6, local copies, waits for them, and re-layouts: 6.12 us -> 0.64 us
    pallas_call x1, Pallas kernels: 21.3 us -> 20.2 us  [local_step(): pl.pallas_call(functools.partial(kernel, sizes), out_shape=(jax.ShapeDtyp...]
    sub x1, other arithmetic: 1.1 us -> 2.12 us  [local_step(): return (residual, state - pace.reshape(1, -1, 1) * residual)]
where the time goes in v2:
time: 23.9 us; the launch traced here: 23.7 us
  Pallas kernels  20.2 us (85%)
  other arithmetic  2.12 us (9%)
  between operations  0.68 us (3%)
  local copies, waits for them, and re-layouts  0.64 us (3%)
    pallas_call x1, Pallas kernels, local_step(): pl.pallas_call(functools.partial(kernel, sizes), out_shape=(jax.ShapeDtyp...  20.2 us
    sub x1, other arithmetic, local_step(): return (residual, state - pace.reshape(1, -1, 1) * residual)  2.12 us
    unnamed x6, local copies, waits for them, and re-layouts  0.64 us

profile of v2, /device:TPU:0, one launch (start us, length us, event | category | flops | bytes accessed | tf_op | source)
XLA Modules:
  0.0 23.7 jit_solution(697357105974648672)
XLA Ops:
  0.6 0.0 copy-start
  0.6 0.0 copy-start.1
  0.7 20.2 %shard_map.122 = (f32[2,256,256]{2,1,0:T(8,128)}, f32[1,256]{1,0:T(1,128)}) custom-call(f32[31]{0:T(128)} %constant.8.clone.lags_hbm, f32[2,256,256]{2,1,0:T(8,128)} %state.1, f32[256,256]{1,0:T(8,128)} %volume_hbm.1, bf16[256,256]{1,0:T(8,128)(2,1)} %constant.11.clone.minus_hbm, bf16[256,384]{1,0:T(8,128)(2,1)} %constant.9.clone.pick_hbm, ...), custom_call_target="tpu_custom_call" | custom-call | flops 3000000000 | bytes 4194304 | tf_op jit(solution)/shard_map/pallas_call | solution.py:309
  20.9 0.0 copy-start.2
  20.9 0.0 copy-done
  20.9 0.0 copy-done.1
  20.9 0.6 %copy-done.2 = f32[1,256]{1,0:T(1,128)S(1)} copy-done((f32[1,256]{1,0:T(1,128)S(1)}, f32[1,256]{1,0:T(1,128)}, u32[]{:S(2)}) %copy-start.2) | copy-done | bytes 1048
  21.6 2.1 %multiply_subtract_fusion = (f32[2,256,256]{2,1,0:T(8,128)}, f32[2,256,256]{2,1,0:T(8,128)}) fusion(f32[2,256,256]{2,1,0:T(8,128)S(1)} %copy-done, f32[256]{0:T(256)S(1)} %bitcast.5, f32[2,256,256]{2,1,0:T(8,128)} %get-tuple-element.4, f32[2,256,256]{2,1,0:T(8,128)S(1)} %copy-done.1), kind=kLoop, calls=%fused_computation | loop fusion | flops 393216 | bytes 2622464 | tf_op jit(solution)/shard_map/sub | solution.py:350
Async XLA Ops:
  0.6 20.3 %copy-start = (f32[2,256,256]{2,1,0:T(8,128)S(1)}, f32[2,256,256]{2,1,0:T(8,128)}, u32[]{:S(2)}) copy-start(f32[2,256,256]{2,1,0:T(8,128)} %state.1) | copy-start | bytes 1572868
  0.6 20.3 %copy-start.1 = (f32[2,256,256]{2,1,0:T(8,128)S(1)}, f32[2,256,256]{2,1,0:T(8,128)}, u32[]{:S(2)}) copy-start(f32[2,256,256]{2,1,0:T(8,128)} %param.12) | copy-start | bytes 1572868
  20.9 0.7 %copy-start.2 = (f32[1,256]{1,0:T(1,128)S(1)}, f32[1,256]{1,0:T(1,128)}, u32[]{:S(2)}) copy-start(f32[1,256]{1,0:T(1,128)} %get-tuple-element.5) | copy-start | bytes 3076

commit v3 on v2

--- a/solution.py
+++ b/solution.py
@@ -107,8 +107,10 @@
         (neighbour_hbm, neighbour), (jscale_hbm, jscale), (left_hbm, send_left), (right_hbm, send_right),
         (state, own), (pick_hbm, pick), (lags_hbm, lags), (volume_hbm, volume_kernel), (minus_hbm, minus),
         (place_hbm, place)))]
-    for one in loads:
+    loads[4].start()
+    for one in loads[:4] + loads[5:]:
         one.start()
+    loads[4].wait()
     pl.semaphore_wait(barrier, len(peers))
 
     def rows(half, cc, k):
@@ -127,7 +129,7 @@
         mate, mate_core = turn(me, d, size), other(core, dc)
         slot = (me, core, k) if sending else (mate, mate_core, k)
         return pltpu.make_async_remote_copy(
-            src_ref=state.at[:, rows(half, mate_core, k)], dst_ref=g.at[slot],
+            src_ref=own.at[:, rows(half, mate_core, k)], dst_ref=g.at[slot],
             send_sem=s.at[mate, mate_core, k], recv_sem=q.at[slot],
             device_id=target(half, mate, fixed, mate_core), device_id_type=MESH)
 
@@ -147,7 +149,7 @@
     for one in firsts:
         first_copy(*one, True).start()
 
-    for one in loads[:5]:
+    for one in loads[:4]:
         one.wait()
     pack[0:6, :] = neighbour[...].astype(F32)
     pack[6:7, :] = jscale[...]
@@ -308,7 +310,7 @@
     sems = pltpu.SemaphoreType.DMA
     term, pace = pl.pallas_call(
         functools.partial(kernel, sizes),
-        out_shape=(jax.ShapeDtypeStruct(state.shape, F32), jax.ShapeDtypeStruct((1, count), F32)),
+        out_shape=(pltpu.VMEM(state.shape, F32), pltpu.VMEM((1, count), F32)),
         in_specs=[pl.BlockSpec(memory_space=pltpu.HBM)] * 10,
         out_specs=[pl.BlockSpec(memory_space=pltpu.VMEM)] * 2,
         scratch_shapes=[

time: 23.9 us -> 21.1 us (0.88)
  other arithmetic: 2.12 us -> 1.1 us
  Pallas kernels: 20.2 us -> 19.2 us
  local copies, waits for them, and re-layouts: 0.64 us -> 0.01 us
    sub x1, other arithmetic: 2.12 us -> 1.1 us  [local_step(): return (residual, state - pace.reshape(1, -1, 1) * residual)]
    pallas_call x1, Pallas kernels: 20.2 us -> 19.2 us  [local_step(): pl.pallas_call(functools.partial(kernel, sizes), out_shape=(pltpu.VMEM(st...]
    unnamed x6 -> x4, local copies, waits for them, and re-layouts: 0.64 us -> 0.01 us
where the time goes in v3:
time: 21.1 us; the launch traced here: 21 us
  Pallas kernels  19.2 us (91%)
  other arithmetic  1.1 us (5%)
  between operations  0.67 us (3%)
    pallas_call x1, Pallas kernels, local_step(): pl.pallas_call(functools.partial(kernel, sizes), out_shape=(pltpu.VMEM(st...  19.2 us
    sub x1, other arithmetic, local_step(): return (residual, state - pace.reshape(1, -1, 1) * residual)  1.1 us

profile of v3, /device:TPU:0, one launch (start us, length us, event | category | flops | bytes accessed | tf_op | source)
XLA Modules:
  0.0 21.0 jit_solution(6232577763188645533)
XLA Ops:
  0.6 0.0 copy-start
  0.6 0.0 copy-start.1
  0.7 19.2 %shard_map.122 = (f32[2,256,256]{2,1,0:T(8,128)S(1)}, f32[1,256]{1,0:T(1,128)S(1)}) custom-call(f32[31]{0:T(128)} %constant.8.clone.lags_hbm, f32[2,256,256]{2,1,0:T(8,128)} %state.1, f32[256,256]{1,0:T(8,128)} %volume_hbm.1, bf16[256,256]{1,0:T(8,128)(2,1)} %constant.11.clone.minus_hbm, bf16[256,384]{1,0:T(8,128)(2,1)} %constant.9.clone.pick_hbm, ...), custom_call_target="tpu_custom_call" | custom-call | flops 3000000000 | bytes 4194304 | tf_op jit(solution)/shard_map/pallas_call | solution.py:311
  19.9 0.0 copy-done
  19.9 0.0 copy-done.1
  19.9 1.1 %multiply_subtract_fusion = (f32[2,256,256]{2,1,0:T(8,128)}, f32[2,256,256]{2,1,0:T(8,128)}) fusion(f32[2,256,256]{2,1,0:T(8,128)S(1)} %copy-done, f32[256]{0:T(256)S(1)} %bitcast.5, f32[2,256,256]{2,1,0:T(8,128)S(1)} %get-tuple-element.4, f32[2,256,256]{2,1,0:T(8,128)S(1)} %copy-done.1), kind=kLoop, calls=%fused_computation | loop fusion | flops 393216 | bytes 2622464 | tf_op jit(solution)/shard_map/sub | solution.py:352
Async XLA Ops:
  0.6 19.2 %copy-start = (f32[2,256,256]{2,1,0:T(8,128)S(1)}, f32[2,256,256]{2,1,0:T(8,128)}, u32[]{:S(2)}) copy-start(f32[2,256,256]{2,1,0:T(8,128)} %state.1) | copy-start | bytes 1572868
  0.6 19.2 %copy-start.1 = (f32[2,256,256]{2,1,0:T(8,128)S(1)}, f32[2,256,256]{2,1,0:T(8,128)}, u32[]{:S(2)}) copy-start(f32[2,256,256]{2,1,0:T(8,128)} %param.12) | copy-start | bytes 1572868

commit v4 on v3

--- a/solution.py
+++ b/solution.py
@@ -1,4 +1,5 @@
 import functools
+import itertools
 
 import jax
 import jax.numpy as jnp
@@ -108,8 +109,6 @@
         (state, own), (pick_hbm, pick), (lags_hbm, lags), (volume_hbm, volume_kernel), (minus_hbm, minus),
         (place_hbm, place)))]
     loads[4].start()
-    for one in loads[:4] + loads[5:]:
-        one.start()
     loads[4].wait()
     pl.semaphore_wait(barrier, len(peers))
 
@@ -144,10 +143,13 @@
 
     firsts = []
     for k in range(chunks):
-        firsts += [(half, step, k) for half in (0, 1) for step in plans[half][0] if step[0]]
+        far = [[(half, step, k) for step in plans[half][0] if step[0]] for half in (0, 1)]
+        firsts += [one for pair in itertools.zip_longest(*far) for one in pair if one]
         firsts += [(half, (0, 1), k) for half in (0, 1)]
     for one in firsts:
         first_copy(*one, True).start()
+    for one in loads[:4] + loads[5:]:
+        one.start()
 
     for one in loads[:4]:
         one.wait()

time: 21.1 us -> 21.2 us (level)
  no operation moved by 1% of the time
where the time goes in v4:
time: 21.2 us; the launch traced here: 21 us
  Pallas kernels  19.2 us (91%)
  other arithmetic  1.1 us (5%)
  between operations  0.67 us (3%)
    pallas_call x1, Pallas kernels, local_step(): pl.pallas_call(functools.partial(kernel, sizes), out_shape=(pltpu.VMEM(st...  19.2 us
    sub x1, other arithmetic, local_step(): return (residual, state - pace.reshape(1, -1, 1) * residual)  1.1 us

profile of v4, /device:TPU:0, one launch (start us, length us, event | category | flops | bytes accessed | tf_op | source)
XLA Modules:
  0.0 21.0 jit_solution(8836804666544907506)
XLA Ops:
  0.6 0.0 copy-start
  0.6 0.0 copy-start.1
  0.7 19.2 %shard_map.122 = (f32[2,256,256]{2,1,0:T(8,128)S(1)}, f32[1,256]{1,0:T(1,128)S(1)}) custom-call(f32[31]{0:T(128)} %constant.8.clone.lags_hbm, f32[2,256,256]{2,1,0:T(8,128)} %state.1, f32[256,256]{1,0:T(8,128)} %volume_hbm.1, bf16[256,256]{1,0:T(8,128)(2,1)} %constant.11.clone.minus_hbm, bf16[256,384]{1,0:T(8,128)(2,1)} %constant.9.clone.pick_hbm, ...), custom_call_target="tpu_custom_call" | custom-call | flops 3000000000 | bytes 4194304 | tf_op jit(solution)/shard_map/pallas_call | solution.py:313
  19.9 0.0 copy-done
  19.9 0.0 copy-done.1
  19.9 1.1 %multiply_subtract_fusion = (f32[2,256,256]{2,1,0:T(8,128)}, f32[2,256,256]{2,1,0:T(8,128)}) fusion(f32[2,256,256]{2,1,0:T(8,128)S(1)} %copy-done, f32[256]{0:T(256)S(1)} %bitcast.5, f32[2,256,256]{2,1,0:T(8,128)S(1)} %get-tuple-element.4, f32[2,256,256]{2,1,0:T(8,128)S(1)} %copy-done.1), kind=kLoop, calls=%fused_computation | loop fusion | flops 393216 | bytes 2622464 | tf_op jit(solution)/shard_map/sub | solution.py:354
Async XLA Ops:
  0.6 19.3 %copy-start = (f32[2,256,256]{2,1,0:T(8,128)S(1)}, f32[2,256,256]{2,1,0:T(8,128)}, u32[]{:S(2)}) copy-start(f32[2,256,256]{2,1,0:T(8,128)} %state.1) | copy-start | bytes 1572868
  0.6 19.3 %copy-start.1 = (f32[2,256,256]{2,1,0:T(8,128)S(1)}, f32[2,256,256]{2,1,0:T(8,128)}, u32[]{:S(2)}) copy-start(f32[2,256,256]{2,1,0:T(8,128)} %param.12) | copy-start | bytes 1572868
